TPU v7x, 32 devices: a whole 2x2x4 slice. The times are simulated.
32 devices in a mesh: dp: 2 (over y), mp: 16 (over z, x, core).
Axes of the slice: x: 2, y: 2, z: 4, core: 2. Of those that a mesh axis runs over, the one named last changes fastest.
Arguments:
- context: bfloat16 [128, 8192], P('dp', 'mp'), may hold values from -6 to 6
- attn_weight: bfloat16 [8192, 5120], P('mp', 'dp'), may hold values from -0.0625 to 0.0625
- stream: bfloat16 [128, 5120], P(('dp', 'mp')), may hold values from -6 to 6
- norm_gain: float32 [5120], replicated, may hold values from 0.1 to 1.9
- router_weight: bfloat16 [16, 5120], replicated, may hold values from -0.078125 to 0.078125
- expert_weights: bfloat16 [16, 3, 1536, 5120], P('mp', None, 'dp'), may hold values from -0.078125 to 0.078125
- inference_slot: int32 [16], replicated, may hold values from 0 to 15, each once
- routes: int32 [128, 6], P(('dp', 'mp')), may hold values from 0 to 15, all different within a row; in each aligned block of 4 rows (0 to 3, 4 to 7, ...) at most 2 rows name the same one
Outputs:
- hidden_out: bfloat16 [128, 5120], P(('dp', 'mp'))
- expert_mix: bfloat16 [128, 5120], P(('dp', 'mp'))
- placed_experts: bfloat16 [16, 3, 1536, 5120], P(None, None, ('dp', 'mp'))
Inputs may be any that keep to these rules, and one draw needn't show every extreme that they name: inference_slot names each position once. `routes`: each row names 6 different experts. Within the rows of one device no expert is named by more than 2 rows, and in every draw some device names some expert exactly 2 times.
All inputs are finite; a program needn't handle non-finite values.
Results may differ from a plain program's by a relative error of at most 0.015.
Values may be sent and summed in bfloat16 or wider, within the bound.
A program may use at most 192 MiB of HBM per device.

v0:
```python
import jax
import jax.numpy as jnp
from jax import lax
from jax.sharding import PartitionSpec as P


def expert_apply(row_block, expert_set):
    contract = (((1,), (1,)), ((), ()))
    gate_part = lax.dot_general(
        row_block, expert_set[0], contract, preferred_element_type=jnp.float32
    )
    up_part = lax.dot_general(
        row_block, expert_set[1], contract, preferred_element_type=jnp.float32
    )
    active = (jax.nn.silu(gate_part) * up_part).astype(jnp.bfloat16)
    return jnp.dot(active, expert_set[2], preferred_element_type=jnp.float32)


def per_device(
    context, attn_weight, stream, norm_gain, router_weight, expert_weights, inference_slot, routes
):
    mp_count = lax.axis_size("mp")
    dp_count = lax.axis_size("dp")
    row_count = stream.shape[0]
    model_width = stream.shape[1]
    top_count = routes.shape[1]
    capacity = max(2, (7 * row_count * top_count + 6 * mp_count - 1) // (6 * mp_count))
    expert_ids = jnp.arange(mp_count, dtype=jnp.int32)
    source = jnp.sum(
        jnp.where(inference_slot[:, None] == expert_ids[None, :], expert_ids[:, None], 0), axis=0
    )
    moved_pieces = lax.all_to_all(expert_weights, "mp", split_axis=2, concat_axis=0, tiled=True)
    placed = jnp.take(moved_pieces, source, axis=0)
    column_width = attn_weight.shape[1]
    partial_value = jnp.dot(
        lax.all_gather(context, "dp", axis=0, tiled=True),
        attn_weight,
        preferred_element_type=jnp.float32,
    )
    partial_value = partial_value.reshape(dp_count, mp_count, row_count, column_width)
    summed = lax.psum_scatter(partial_value, "mp", scatter_dimension=1, tiled=True).reshape(
        dp_count, row_count, column_width
    )
    attended = lax.all_to_all(summed, "dp", split_axis=0, concat_axis=2, tiled=True).reshape(
        row_count, model_width
    )
    hidden = (stream.astype(jnp.float32) + attended).astype(jnp.bfloat16)
    widened = hidden.astype(jnp.float32)
    normed = (
        widened * lax.rsqrt(jnp.mean(widened * widened, axis=1, keepdims=True) + 1e-06) * norm_gain
    ).astype(jnp.bfloat16)
    logits = lax.dot_general(
        normed, router_weight, (((1,), (1,)), ((), ())), preferred_element_type=jnp.float32
    )
    scores = jax.nn.sigmoid(logits)
    matches = routes[:, :, None] == expert_ids[None, None, :]
    chosen = jnp.sum(jnp.where(matches, scores[:, None, :], 0.0), axis=2)
    share = 2.5 * chosen / jnp.sum(chosen, axis=1, keepdims=True)
    destination = jnp.sum(jnp.where(matches, source[None, None, :], 0), axis=2).reshape(-1)
    onehot = (destination[:, None] == expert_ids[None, :]).astype(jnp.int32)
    earlier = jnp.cumsum(onehot, axis=0) - onehot
    position = jnp.sum(earlier * onehot, axis=1)
    slot_index = destination * capacity + position
    slot_ids = jnp.arange(mp_count * capacity, dtype=jnp.int32)
    placing = (slot_index[:, None] == slot_ids[None, :]).astype(jnp.float32)
    row_ids = jnp.arange(row_count * top_count, dtype=jnp.int32) // top_count
    row_owner = (row_ids[:, None] == jnp.arange(row_count, dtype=jnp.int32)[None, :]).astype(
        jnp.float32
    )
    pick_matrix = jnp.dot(placing.T, row_owner, precision=lax.Precision.HIGHEST).astype(
        jnp.bfloat16
    )
    outgoing = jnp.dot(pick_matrix, normed, preferred_element_type=jnp.float32).astype(jnp.bfloat16)
    outgoing = outgoing.reshape(mp_count, capacity, model_width)
    combine_matrix = jnp.dot(
        row_owner.T, placing * share.reshape(-1)[:, None], precision=lax.Precision.HIGHEST
    )
    local_expert = expert_weights[0]
    copies = jnp.broadcast_to(outgoing[None], (dp_count,) + outgoing.shape).reshape(
        dp_count * mp_count, capacity, model_width
    )
    arrived = lax.all_to_all(copies, ("dp", "mp"), split_axis=0, concat_axis=0, tiled=True)
    partial_out = (
        expert_apply(arrived.reshape(-1, model_width), local_expert)
        .astype(jnp.bfloat16)
        .reshape(arrived.shape)
    )
    returned = lax.all_to_all(partial_out, ("dp", "mp"), split_axis=0, concat_axis=0, tiled=True)
    returned = returned.reshape(dp_count, mp_count, capacity, model_width)
    results = jnp.sum(returned, axis=0, dtype=jnp.float32).astype(jnp.bfloat16)
    expert_mix = jnp.dot(
        combine_matrix,
        results.reshape(-1, model_width).astype(jnp.float32),
        precision=lax.Precision.HIGHEST,
    ).astype(jnp.bfloat16)
    return (hidden, expert_mix, placed)


def solution(mesh):
    placed = (
        P("dp", "mp"),
        P("mp", "dp"),
        P(("dp", "mp"), None),
        P(),
        P(),
        P("mp", None, "dp", None),
        P(),
        P(("dp", "mp"), None),
    )
    return jax.shard_map(
        per_device,
        mesh=mesh,
        in_specs=placed,
        out_specs=(P(("dp", "mp"), None), P(("dp", "mp"), None), P(None, None, ("dp", "mp"), None)),
        check_vma=False,
    )
```

profile of v0, /device:TPU:11, one launch (start us, length us, event | category | flops | bytes accessed | tf_op | source)
XLA Modules:
  0.0 955.9 jit_solution(12595654213879509104)
XLA Ops:
  7.2 4.1 all_gather.3
  11.4 1.6 fusion.46
  12.9 2.6 reshape.110
  15.6 0.8 copy.18
  17.6 1.2 dynamic-slice
  19.1 91.0 %all-reduce.3.cloned.1.call-done = f32[2,16,4,2560]{3,2,1,0:T(4,128)} async-done(((f32[2,16,4,2560]{3,2,1,0:T(4,128)}), f32[2,16,4,2560]{3,2,1,0:T(4,128)}) %all-reduce.3.cloned.1.call-update) | async-done | bytes 1310736
  110.1 2.2 dynamic-slice_bitcast_fusion
  112.3 3.3 all-to-all-start
  115.9 2.8 all-to-all-done
  118.7 0.9 fusion.29
  119.6 1.0 convolution_convert_fusion
  121.1 23.3 %all_to_all.43 = bf16[32,2,5120]{2,1,0:T(2,128)(2,1)S(1)} all-to-all(bf16[32,2,5120]{2,1,0:T(2,128)(2,1)S(1)} %bitcast.49), channel_id=1, replica_groups=mesh['dp'=2,'mp'=16] {'dp','mp'}, dimensions={0} | all-to-all | bytes 1310720 | tf_op jit(solution)/shard_map/all_to_all | solution.py:82
  144.7 5.7 fusion.4
  150.4 10.4 %fusion.9 = bf16[64,5120]{1,0:T(8,128)(2,1)S(1)} fusion(bf16[1,3,768,5120]{3,2,1,0:T(8,128)(2,1)} %param.13, bf16[64,5120]{1,0:T(8,128)(2,1)S(1)} %reshape.115, f32[64,768]{1,0:T(8,128)S(1)} %fusion.4), kind=kOutput, calls=%fused_computation.12 | convolution fusion | flops 1007255552 | bytes 17235968 | tf_op jit(solution)/shard_map/dot_general | solution.py:16
  160.8 1.1 reshape.116
  161.9 4.5 all-to-all-start.2
  166.4 35.7 %copy.21 = bf16[1,3,768,5120]{3,1,0,2:T(4,128)(2,1)} copy(bf16[1,3,768,5120]{3,2,1,0:T(8,128)(2,1)} %param.13) | data formatting | bytes 47185920 | tf_op args[5]
  202.1 6.3 all-to-all-start.3
  209.4 1.4 reduce_sum.74
  210.9 0.9 convolution_convert_fusion.1
  211.8 673.3 %all-to-all-done.3 = bf16[1,3,768,5120]{3,1,0,2:T(4,128)(2,1)} async-done(((bf16[1,3,768,5120]{3,1,0,2:T(4,128)(2,1)}), bf16[1,3,768,5120]{3,1,0,2:T(4,128)(2,1)}, u32[]{:S(2)}, u32[]{:S(2)}) %all-to-all-start.3) | async-done | bytes 23592992 | tf_op jit(solution)/shard_map/all_to_all | solution.py:32
  885.1 26.3 %copy.29 = bf16[1,3,16,48,5120]{4,3,1,2,0:T(8,128)(2,1)} copy(bf16[1,3,16,48,5120]{4,1,3,2,0:T(4,128)(2,1)} %bitcast.9) | data formatting | bytes 47185920 | tf_op jit(solution)/shard_map/all_to_all | solution.py:32
  911.4 17.4 %gather_fusion = bf16[16,3,48,5120]{3,2,1,0:T(8,128)(2,1)} fusion(bf16[16,3,48,5120]{3,2,1,0:T(8,128)(2,1)} %bitcast.47, s32[1024]{0:T(1024)S(1)} %pad_clamp_fusion), kind=kCustom, calls=%fused_computation | custom fusion | bytes 47185984 | tf_op jit(solution)/shard_map/jit(_take)/gather | solution.py:33
  928.9 20.2 %broadcast_select_fusion = bf16[16,3,48,5120]{3,2,1,0:T(8,128)(2,1)} fusion(bf16[16,3,48,5120]{3,2,1,0:T(8,128)(2,1)} %gather_fusion, pred[16]{0:T(512)(128)(4,1)S(1)} %compare_and_fusion), kind=kLoop, calls=%fused_computation.2 | loop fusion | flops 11796480 | bytes 47185936 | tf_op jit(solution)/shard_map/jit(_take)/select_n | solution.py:33
  (36 shorter events, 3.6 us)
Async XLA Ops:
  7.2 4.2 copy-start
  7.2 102.9 %all-reduce.3.cloned.1.call-start = ((), (), s32[]{:S(2)}) async-start(), calls=%async_computation.4 | async-start | bytes 2621440
  112.3 6.4 all-to-all-start
  119.6 88.9 %copy-start.2 = (bf16[4,5120]{1,0:T(4,128)(2,1)}, bf16[4,5120]{1,0:T(4,128)(2,1)S(1)}, u32[]{:S(2)}) copy-start(bf16[4,5120]{1,0:T(4,128)(2,1)S(1)} %get-tuple-element.6) | copy-start | bytes 122884
  161.9 40.2 %all-to-all-start.2 = ((bf16[32,2,5120]{2,1,0:T(2,128)(2,1)}), bf16[32,2,5120]{2,1,0:T(2,128)(2,1)S(1)}, u32[]{:S(2)}, u32[]{:S(2)}) async-start(bf16[32,2,5120]{2,1,0:T(2,128)(2,1)} %reshape.116), calls=%async_computation.2 | async-start | bytes 1310720 | tf_op jit(solution)/shard_map/all_to_all | solution.py:88
  202.1 6.4 copy-start.3
  202.1 6.4 copy-start.4
  202.1 683.0 %all-to-all-start.3 = ((bf16[1,3,768,5120]{3,1,0,2:T(4,128)(2,1)}), bf16[1,3,768,5120]{3,1,0,2:T(4,128)(2,1)}, u32[]{:S(2)}, u32[]{:S(2)}) async-start(bf16[1,3,768,5120]{3,1,0,2:T(4,128)(2,1)} %copy.21), calls=%async_computation.3 | async-start | bytes 62914560 | tf_op jit(solution)/shard_map/all_to_all | solution.py:32
  911.4 37.7 %copy-start.1 = (bf16[512,2560]{1,0:T(8,128)(2,1)S(1)}, bf16[512,2560]{1,0:T(8,128)(2,1)}, u32[]{:S(2)}) copy-start(bf16[512,2560]{1,0:T(8,128)(2,1)} %param.9) | copy-start | bytes 7864324
Sparse Core Ops, SparseCore 0:
  15.7 94.3 all-reduce.2
where the time goes:
time: 957 us; the launch traced here: 956 us
  waiting for transfers between devices  767 us (80%)
  local copies, waits for them, and re-layouts  88.5 us (9%)
  blocking collectives  27.4 us (3%)
  other arithmetic  24.1 us (3%)
  matrix products  20.4 us (2%)
  starting transfers between devices  14.2 us (1%)
  between operations  14.2 us (1%)
    all_to_all x1, waiting for transfers between devices, per_device(): lax.all_to_all(expert_weights, 'mp', split_axis=2, concat_axis=0, tiled=T...  673 us
    unnamed x2, waiting for transfers between devices  91 us
    unnamed x13, local copies, waits for them, and re-layouts  37.7 us
    all_to_all x1, local copies, waits for them, and re-layouts, per_device(): lax.all_to_all(expert_weights, 'mp', split_axis=2, concat_axis=0, tiled=T...  26.3 us
    all_to_all x1, blocking collectives, per_device(): lax.all_to_all(copies, ('dp', 'mp'), split_axis=0, concat_axis=0, tiled=T...  23.3 us
    select_n x2, other arithmetic, per_device(): placed = jnp.take(moved_pieces, source, axis=0)  20.3 us
  transfers between devices with their start and end apart: 4, of which 3 were waited for; matrix products, arithmetic and copies ran while one was open for 4% of the time, Pallas kernels for 0%

commit v1 on v0

v1 whole, which is shorter than its diff:
```python
import functools

import jax
import jax.numpy as jnp
from jax import lax
from jax.experimental import pallas as pl
from jax.experimental.pallas import tpu as pltpu
from jax.sharding import PartitionSpec as P

MESH = pl.DeviceIdType.MESH
PARTS = ((0, 1), (2,))


def offsets(count):
    half = count // 2
    order = [half]
    for step in range(1, half):
        order += [half - step, half + step]
    return [value for value in order if 0 < value < count]


def move_kernel(parts, first, *refs):
    weights, moved, send_sem, recv_sem, own_sem = refs if first else (refs[0],) + refs[2:]
    count = weights.shape[1]
    me, row = lax.axis_index("mp"), lax.axis_index("dp")
    barrier = pltpu.get_barrier_semaphore()
    for step in range(1, count):
        pl.semaphore_signal(
            barrier, inc=1, device_id=(row, lax.rem(me + step, count)), device_id_type=MESH
        )
    pl.semaphore_wait(barrier, count - 1)
    copies = []
    for step in offsets(count):
        peer = lax.rem(me + step, count)
        for at, part in enumerate(parts):
            copy = pltpu.make_async_remote_copy(
                src_ref=weights.at[part, peer],
                dst_ref=moved.at[me, part],
                send_sem=send_sem.at[at, step],
                recv_sem=recv_sem.at[at, step],
                device_id=(row, peer),
                device_id_type=MESH,
            )
            copy.start()
            copies.append(copy)
    own = []
    for at, part in enumerate(parts):
        copy = pltpu.make_async_copy(weights.at[part, me], moved.at[me, part], own_sem.at[at])
        copy.start()
        own.append(copy)
    for copy in own:
        copy.wait()
    for copy in copies:
        copy.wait_send()
    for copy in copies:
        copy.wait_recv()


def move(weights, held, parts, number):
    _, count, rows, width = weights.shape
    out = jax.ShapeDtypeStruct((count, 3, rows, width), weights.dtype)
    operands = (weights,) if held is None else (weights, held)
    size = len(parts) * count * rows * width * 2
    return pl.pallas_call(
        functools.partial(move_kernel, parts, held is None),
        out_shape=out,
        in_specs=[pl.BlockSpec(memory_space=pl.ANY)] * len(operands),
        out_specs=pl.BlockSpec(memory_space=pl.ANY),
        input_output_aliases={} if held is None else {1: 0},
        scratch_shapes=[
            pltpu.SemaphoreType.DMA((len(parts), count)),
            pltpu.SemaphoreType.DMA((len(parts), count)),
            pltpu.SemaphoreType.DMA((len(parts),)),
        ],
        compiler_params=pltpu.CompilerParams(collective_id=number, has_side_effects=True),
        cost_estimate=pl.CostEstimate(flops=0, bytes_accessed=size * 80, transcendentals=0),
    )(*operands)


def place_kernel(source_ref, moved_ref, out_ref):
    out_ref[...] = moved_ref[...]


def place(moved, source):
    count, three, rows, width = moved.shape
    return pl.pallas_call(
        place_kernel,
        out_shape=jax.ShapeDtypeStruct(moved.shape, moved.dtype),
        grid_spec=pltpu.PrefetchScalarGridSpec(
            num_scalar_prefetch=1,
            grid=(count,),
            in_specs=[
                pl.BlockSpec((1, three, rows, width), lambda i, source_ref: (source_ref[i], 0, 0, 0))
            ],
            out_specs=pl.BlockSpec((1, three, rows, width), lambda i, source_ref: (i, 0, 0, 0)),
        ),
        compiler_params=pltpu.CompilerParams(vmem_limit_bytes=24 * 2**20),
    )(source, moved)


def per_device(
    context, attn_weight, stream, norm_gain, router_weight, expert_weights, inference_slot, routes
):
    mp_count = lax.axis_size("mp")
    dp_count = lax.axis_size("dp")
    row_count, model_width = stream.shape
    me = lax.axis_index("mp")
    expert_ids = jnp.arange(mp_count, dtype=jnp.int32)
    named = inference_slot[:, None] == expert_ids[None, :]
    source = jnp.sum(jnp.where(named, expert_ids[:, None], 0), axis=0)
    hidden_units = expert_weights.shape[2]
    weights = expert_weights.reshape(3, mp_count, hidden_units // mp_count, model_width)
    column_width = attn_weight.shape[1]
    capacity = max(2, (7 * row_count * routes.shape[1] + 6 * mp_count - 1) // (6 * mp_count))

    whole_context = lax.all_gather(context, "dp", axis=0, tiled=True)
    partial_value = jnp.dot(whole_context, attn_weight, preferred_element_type=jnp.float32)
    partial_value = partial_value.astype(jnp.bfloat16).reshape(-1, row_count, column_width)
    spread = lax.all_to_all(partial_value, ("dp", "mp"), split_axis=0, concat_axis=0, tiled=True)
    attended = jnp.sum(
        spread.astype(jnp.float32).reshape(dp_count, mp_count, row_count, column_width), axis=1
    )
    attended = jnp.swapaxes(attended, 0, 1).reshape(row_count, model_width)
    hidden = (stream.astype(jnp.float32) + attended).astype(jnp.bfloat16)
    widened = hidden.astype(jnp.float32)
    normed = (
        widened * lax.rsqrt(jnp.mean(widened * widened, axis=1, keepdims=True) + 1e-06) * norm_gain
    ).astype(jnp.bfloat16)
    wide_ids = jnp.arange(-(-mp_count // 128) * 128, dtype=jnp.int32)
    naming = jnp.any(routes[:, :, None] == wide_ids[None, None, :], axis=1).astype(jnp.bfloat16)
    packet = jnp.concatenate([normed, naming], axis=1)
    packet, weights = lax.optimization_barrier((packet, weights))
    packets = lax.all_gather(packet, ("dp", "mp"), axis=0, tiled=True)
    moved = move(weights, None, PARTS[0], 0)
    packets, moved = lax.optimization_barrier((packets, moved))

    contract = (((1,), (1,)), ((), ()))
    mine = inference_slot[me] == expert_ids
    named_mine = jnp.any(
        (packets[:, model_width : model_width + mp_count] > 0) & mine[None, :], axis=1
    ).reshape(-1, row_count)
    picks = slot_picks(named_mine, capacity)
    groups = named_mine.shape[0]
    same = jnp.arange(groups)[:, None] == jnp.arange(groups)[None, :]
    picking = (same[:, None, :, None] & picks[:, :, None, :]).reshape(
        groups * capacity, groups * row_count
    )
    rows = jnp.dot(
        picking.astype(jnp.bfloat16),
        packets[:, :model_width],
        preferred_element_type=jnp.float32,
    ).astype(jnp.bfloat16)
    experts = expert_weights[0]
    gate = lax.dot_general(rows, experts[0], contract, preferred_element_type=jnp.float32)
    up = lax.dot_general(rows, experts[1], contract, preferred_element_type=jnp.float32)
    active = (jax.nn.silu(gate) * up).astype(jnp.bfloat16)
    answers = jnp.dot(active, experts[2], preferred_element_type=jnp.float32)
    answers = answers.astype(jnp.bfloat16).reshape(groups, capacity, model_width)
    returned = lax.all_to_all(answers, ("dp", "mp"), split_axis=0, concat_axis=0, tiled=True)
    returned, moved = lax.optimization_barrier((returned, moved))
    moved = move(weights, moved, PARTS[1], 1)

    logits = lax.dot_general(normed, router_weight, contract, preferred_element_type=jnp.float32)
    matches = naming[:, :mp_count] > 0
    chosen = jnp.where(matches, jax.nn.sigmoid(logits), 0.0)
    share = 2.5 * chosen / jnp.sum(chosen, axis=1, keepdims=True)
    by_holder = jnp.sum(
        jnp.where(named[:, None, :], share[None], 0.0), axis=2
    )
    holder_picks = slot_picks(
        jnp.any(named[:, None, :] & matches[None], axis=2), capacity
    )
    mixing = jnp.where(holder_picks, by_holder[:, None, :], 0.0).reshape(-1, row_count)
    results = jnp.sum(
        returned.astype(jnp.float32).reshape(dp_count, -1, model_width), axis=0
    )
    mix = jnp.dot(mixing.T, results, precision=lax.Precision.HIGHEST).astype(jnp.bfloat16)
    return (hidden, mix, place(moved, source))


def slot_picks(named, capacity):
    count = named.astype(jnp.int32)
    width = named.shape[1]
    before = jnp.arange(width)[:, None] < jnp.arange(width)[None, :]
    position = jnp.sum(jnp.where(before[None], count[:, :, None], 0), axis=1)
    return named[:, None, :] & (position[:, None, :] == jnp.arange(capacity)[None, :, None])


def solution(mesh):
    placed = (
        P("dp", "mp"),
        P("mp", "dp"),
        P(("dp", "mp"), None),
        P(),
        P(),
        P("mp", None, "dp", None),
        P(),
        P(("dp", "mp"), None),
    )
    return jax.shard_map(
        per_device,
        mesh=mesh,
        in_specs=placed,
        out_specs=(P(("dp", "mp"), None), P(("dp", "mp"), None), P(None, None, ("dp", "mp"), None)),
        check_vma=False,
    )
```

time: 957 us -> 635 us (0.66)
  waiting for transfers between devices: 767 us -> 31.1 us
  Pallas kernels: 0 us -> 535 us
  local copies, waits for them, and re-layouts: 88.5 us -> 16.2 us
  blocking collectives: 27.4 us -> 4.14 us
  other arithmetic: 24.1 us -> 4.64 us
    all_to_all x3 -> x2, waiting for transfers between devices: 676 us -> 31.1 us  [the longest x1 15.8 us: per_device(): lax.all_to_all(partial_value, ('dp', 'mp'), split_axis=0, concat_axis=0,...]
    pallas_call x0 -> x3, Pallas kernels: none -> 535 us  [the longest x2 524 us: move(): pl.pallas_call(functools.partial(move_kernel, parts, held is None), out_s...]
    unnamed x2 -> x1, waiting for transfers between devices: 91 us -> 0.02 us
    unnamed x13, local copies, waits for them, and re-layouts: 37.7 us -> 8.5 us
    all_to_all x1 -> x0, local copies, waits for them, and re-layouts: 26.3 us -> none  [per_device(): lax.all_to_all(expert_weights, 'mp', split_axis=2, concat_axis=0, tiled=T...]
    all_to_all x1 -> x0, blocking collectives: 23.3 us -> none  [per_device(): lax.all_to_all(copies, ('dp', 'mp'), split_axis=0, concat_axis=0, tiled=T...]
    select_n x3 -> x0, other arithmetic: 20.3 us -> none  [the longest x2 20.3 us: per_device(): placed = jnp.take(moved_pieces, source, axis=0)]
    gather x1 -> x0, local copies, waits for them, and re-layouts: 17.4 us -> none  [per_device(): placed = jnp.take(moved_pieces, source, axis=0)]
  transfers between devices with their start and end apart: 4 -> 3, of which waited for: 3 -> 2; matrix products, arithmetic and copies ran while one was open for 4% -> 1% of each run, Pallas kernels for 0% -> 55%
where the time goes in v1:
time: 635 us; the launch traced here: 634 us
  Pallas kernels  535 us (84%)
  waiting for transfers between devices  31.1 us (5%)
  matrix products  18.4 us (3%)
  local copies, waits for them, and re-layouts  16.2 us (3%)
  between operations  14.3 us (2%)
  starting transfers between devices  10.4 us (2%)
    pallas_call x2, Pallas kernels, move(): pl.pallas_call(functools.partial(move_kernel, parts, held is None), out_s...  524 us
    all_to_all x1, waiting for transfers between devices, per_device(): lax.all_to_all(partial_value, ('dp', 'mp'), split_axis=0, concat_axis=0,...  15.8 us
    all_to_all x1, waiting for transfers between devices, per_device(): lax.all_to_all(answers, ('dp', 'mp'), split_axis=0, concat_axis=0, tiled=...  15.2 us
  transfers between devices with their start and end apart: 3, of which 2 were waited for; matrix products, arithmetic and copies ran while one was open for 1% of the time, Pallas kernels for 55%

profile of v1, /device:TPU:11, one launch (start us, length us, event | category | flops | bytes accessed | tf_op | source)
XLA Modules:
  0.0 634.1 jit_solution(11053075135838703224)
XLA Ops:
  7.2 4.1 all_gather.6
  11.3 0.5 convolution_convert_fusion.2
  11.8 1.0 reshape.121
  12.8 7.5 %all-to-all-start = ((bf16[32,4,2560]{2,1,0:T(4,128)(2,1)}), bf16[32,4,2560]{2,1,0:T(4,128)(2,1)S(1)}, u32[]{:S(2)}, u32[]{:S(2)}) async-start(bf16[32,4,2560]{2,1,0:T(4,128)(2,1)} %reshape.121), calls=%async_computation | async-start | bytes 1310720 | tf_op jit(solution)/shard_map/all_to_all | solution.py:119
  20.4 0.8 copy.21
  21.2 15.8 %all-to-all-done = bf16[32,4,2560]{2,1,0:T(4,128)(2,1)S(1)} async-done(((bf16[32,4,2560]{2,1,0:T(4,128)(2,1)}), bf16[32,4,2560]{2,1,0:T(4,128)(2,1)S(1)}, u32[]{:S(2)}, u32[]{:S(2)}) %all-to-all-start) | async-done | bytes 655392 | tf_op jit(solution)/shard_map/all_to_all | solution.py:119
  37.4 0.9 fusion.31
  38.3 0.8 fusion.33
  39.1 0.6 pad_maximum_fusion
  39.8 1.2 dynamic_slice.3
  41.1 0.6 iota_compare_fusion.4
  41.7 349.8 %shard_map.103.refs_1_ = bf16[16,3,48,5120]{3,2,1,0:T(8,128)(2,1)} custom-call(bf16[3,16,48,5120]{3,2,1,0:T(8,128)(2,1)} %bitcast.40), custom_call_target="tpu_custom_call" | custom-call | bytes 1258291200 | tf_op jit(solution)/shard_map/pallas_call | solution.py:64
  391.6 2.5 reshape.134
  394.8 0.8 and.78
  395.6 0.3 convolution_convert_fusion
  395.9 5.7 fusion.4
  401.7 10.5 %fusion.9 = bf16[64,5120]{1,0:T(8,128)(2,1)S(1)} fusion(bf16[1,3,768,5120]{3,2,1,0:T(8,128)(2,1)} %param.13, bf16[64,5120]{1,0:T(8,128)(2,1)S(1)} %convolution_convert_fusion, f32[64,768]{1,0:T(8,128)S(1)} %fusion.4), kind=kOutput, calls=%fused_computation.9 | convolution fusion | flops 1007255552 | bytes 17235968 | tf_op jit(solution)/shard_map/dot_general | solution.py:157
  412.2 1.1 reshape.126
  413.3 2.9 all-to-all-start.1
  417.7 15.2 %all-to-all-done.1 = bf16[32,2,5120]{2,1,0:T(2,128)(2,1)S(1)} async-done(((bf16[32,2,5120]{2,1,0:T(2,128)(2,1)}), bf16[32,2,5120]{2,1,0:T(2,128)(2,1)S(1)}, u32[]{:S(2)}, u32[]{:S(2)}) %all-to-all-start.1) | async-done | bytes 655392 | tf_op jit(solution)/shard_map/all_to_all | solution.py:159
  433.1 174.6 %shard_map.104.moved_ref = bf16[16,3,48,5120]{3,2,1,0:T(8,128)(2,1)} custom-call(bf16[3,16,48,5120]{3,2,1,0:T(8,128)(2,1)} %bitcast.41, bf16[16,3,48,5120]{3,2,1,0:T(8,128)(2,1)} %shard_map.103.refs_1_), custom_call_target="tpu_custom_call", output_to_operand_aliasing={{}: (1, {})} | custom-call | bytes 629145600 | tf_op jit(solution)/shard_map/pallas_call | solution.py:64
  607.8 7.7 %copy-done.2 = bf16[16,3,48,5120]{3,2,1,0:T(8,128)(2,1)S(1)} copy-done((bf16[16,3,48,5120]{3,2,1,0:T(8,128)(2,1)S(1)}, bf16[16,3,48,5120]{3,2,1,0:T(8,128)(2,1)}, u32[]{:S(2)}) %copy-start.2) | copy-done | bytes 23592984
  615.5 10.7 %shard_map.105 = bf16[16,3,48,5120]{3,2,1,0:T(8,128)(2,1)} custom-call(s32[16]{0:T(128)S(1)} %select_reduce_fusion.1.source_ref, bf16[16,3,48,5120]{3,2,1,0:T(8,128)(2,1)S(1)} %copy-done.2), custom_call_target="tpu_custom_call" | custom-call | tf_op jit(solution)/shard_map/pallas_call | solution.py:86
  626.2 1.0 convolution_convert_fusion.1
  (49 shorter events, 3.1 us)
Async XLA Ops:
  7.2 4.2 copy-start
  12.8 24.3 %all-to-all-start = ((bf16[32,4,2560]{2,1,0:T(4,128)(2,1)}), bf16[32,4,2560]{2,1,0:T(4,128)(2,1)S(1)}, u32[]{:S(2)}, u32[]{:S(2)}) async-start(bf16[32,4,2560]{2,1,0:T(4,128)(2,1)} %reshape.121), calls=%async_computation | async-start | bytes 1310720 | tf_op jit(solution)/shard_map/all_to_all | solution.py:119
  20.3 371.2 %all-gather.3.cloned.1.call-start = ((), (), s32[]{:S(2)}) async-start(), calls=%async_computation.2 | async-start | bytes 1385472 | tf_op jit(solution)/shard_map/all_gather | solution.py:133
  38.3 353.2 %copy-start.3 = (bf16[4,5120]{1,0:T(4,128)(2,1)}, bf16[4,5120]{1,0:T(4,128)(2,1)S(1)}, u32[]{:S(2)}) copy-start(bf16[4,5120]{1,0:T(4,128)(2,1)S(1)} %get-tuple-element.16) | copy-start | bytes 122884
  401.7 14.5 %copy-start.4 = (s32[16]{0:T(128)S(1)}, s32[16]{0:T(128)}, u32[]{:S(2)}) copy-start(s32[16]{0:T(128)} %param.14) | copy-start | bytes 196
  401.7 15.3 %copy-start.5 = (bf16[16,5120]{1,0:T(8,128)(2,1)S(1)}, bf16[16,5120]{1,0:T(8,128)(2,1)}, u32[]{:S(2)}) copy-start(bf16[16,5120]{1,0:T(8,128)(2,1)} %param.12) | copy-start | bytes 491524
  413.3 19.6 %all-to-all-start.1 = ((bf16[32,2,5120]{2,1,0:T(2,128)(2,1)}), bf16[32,2,5120]{2,1,0:T(2,128)(2,1)S(1)}, u32[]{:S(2)}, u32[]{:S(2)}) async-start(bf16[32,2,5120]{2,1,0:T(2,128)(2,1)} %reshape.126), calls=%async_computation.1 | async-start | bytes 1310720 | tf_op jit(solution)/shard_map/all_to_all | solution.py:159
  607.8 7.7 %copy-start.2 = (bf16[16,3,48,5120]{3,2,1,0:T(8,128)(2,1)S(1)}, bf16[16,3,48,5120]{3,2,1,0:T(8,128)(2,1)}, u32[]{:S(2)}) copy-start(bf16[16,3,48,5120]{3,2,1,0:T(8,128)(2,1)} %shard_map.104.moved_ref) | copy-start | bytes 70778880
  615.5 11.7 %copy-start.1 = (bf16[512,2560]{1,0:T(8,128)(2,1)S(1)}, bf16[512,2560]{1,0:T(8,128)(2,1)}, u32[]{:S(2)}) copy-start(bf16[512,2560]{1,0:T(8,128)(2,1)} %param.9) | copy-start | bytes 7864324
Sparse Core Ops, SparseCore 0:
  39.9 284.7 all-gather.2

commit v2 on v1

--- a/solution.py
+++ b/solution.py
@@ -19,9 +19,9 @@
     return [value for value in order if 0 < value < count]
 
 
-def move_kernel(parts, first, *refs):
-    weights, moved, send_sem, recv_sem, own_sem = refs if first else (refs[0],) + refs[2:]
+def move_kernel(parts, ahead, weights, early, moved, send_sem, recv_sem, own_sem):
     count = weights.shape[1]
+    half = count // 2
     me, row = lax.axis_index("mp"), lax.axis_index("dp")
     barrier = pltpu.get_barrier_semaphore()
     for step in range(1, count):
@@ -33,9 +33,11 @@
     for step in offsets(count):
         peer = lax.rem(me + step, count)
         for at, part in enumerate(parts):
+            if part == ahead and step == half:
+                continue
             copy = pltpu.make_async_remote_copy(
                 src_ref=weights.at[part, peer],
-                dst_ref=moved.at[me, part],
+                dst_ref=moved.at[me, at],
                 send_sem=send_sem.at[at, step],
                 recv_sem=recv_sem.at[at, step],
                 device_id=(row, peer),
@@ -45,9 +47,16 @@
             copies.append(copy)
     own = []
     for at, part in enumerate(parts):
-        copy = pltpu.make_async_copy(weights.at[part, me], moved.at[me, part], own_sem.at[at])
+        own.append(pltpu.make_async_copy(weights.at[part, me], moved.at[me, at], own_sem.at[at]))
+    own.append(
+        pltpu.make_async_copy(
+            early,
+            moved.at[lax.rem(me + count - half, count), parts.index(ahead)],
+            own_sem.at[len(parts)],
+        )
+    )
+    for copy in own:
         copy.start()
-        own.append(copy)
     for copy in own:
         copy.wait()
     for copy in copies:
@@ -56,46 +65,65 @@
         copy.wait_recv()
 
 
-def move(weights, held, parts, number):
+def move(weights, early, parts, number):
     _, count, rows, width = weights.shape
-    out = jax.ShapeDtypeStruct((count, 3, rows, width), weights.dtype)
-    operands = (weights,) if held is None else (weights, held)
     size = len(parts) * count * rows * width * 2
     return pl.pallas_call(
-        functools.partial(move_kernel, parts, held is None),
-        out_shape=out,
-        in_specs=[pl.BlockSpec(memory_space=pl.ANY)] * len(operands),
+        functools.partial(move_kernel, parts, parts[0]),
+        out_shape=jax.ShapeDtypeStruct((count, len(parts), rows, width), weights.dtype),
+        in_specs=[pl.BlockSpec(memory_space=pl.ANY)] * 2,
         out_specs=pl.BlockSpec(memory_space=pl.ANY),
-        input_output_aliases={} if held is None else {1: 0},
         scratch_shapes=[
             pltpu.SemaphoreType.DMA((len(parts), count)),
             pltpu.SemaphoreType.DMA((len(parts), count)),
-            pltpu.SemaphoreType.DMA((len(parts),)),
+            pltpu.SemaphoreType.DMA((len(parts) + 1,)),
         ],
         compiler_params=pltpu.CompilerParams(collective_id=number, has_side_effects=True),
         cost_estimate=pl.CostEstimate(flops=0, bytes_accessed=size * 80, transcendentals=0),
-    )(*operands)
-
-
-def place_kernel(source_ref, moved_ref, out_ref):
-    out_ref[...] = moved_ref[...]
-
-
-def place(moved, source):
-    count, three, rows, width = moved.shape
+    )(weights, early)
+
+
+def cut_piece(weights, part):
+    _, count, rows, width = weights.shape
+    peer = lax.rem(lax.axis_index("mp") + count // 2, count)
+    start = (jnp.int32(part), peer, jnp.int32(0), jnp.int32(0))
+    return lax.dynamic_slice(weights, start, (1, 1, rows, width)).reshape(rows, width)
+
+
+def send_ahead(piece):
+    count = lax.axis_size("mp")
+    half = count // 2
+    return lax.ppermute(piece, "mp", [(i, (i + half) % count) for i in range(count)])
+
+
+def place_kernel(*refs):
+    moved_ref, out_ref = refs[1], refs[-1]
+    out_ref[:, 0] = moved_ref[:, 0]
+
+
+def place(moved, source, parts, held):
+    count, number, rows, width = moved.shape
+    first = parts[0]
+    block = (1, 1, rows, width)
+    operands = (source, moved) if held is None else (source, moved, held)
+    in_specs = [pl.BlockSpec(block, lambda i, p, source_ref: (source_ref[i], p, 0, 0))]
+    if held is not None:
+        in_specs.append(pl.BlockSpec(memory_space=pl.ANY))
     return pl.pallas_call(
         place_kernel,
-        out_shape=jax.ShapeDtypeStruct(moved.shape, moved.dtype),
+        out_shape=jax.ShapeDtypeStruct((count, 3, rows, width), moved.dtype),
         grid_spec=pltpu.PrefetchScalarGridSpec(
             num_scalar_prefetch=1,
-            grid=(count,),
-            in_specs=[
-                pl.BlockSpec((1, three, rows, width), lambda i, source_ref: (source_ref[i], 0, 0, 0))
-            ],
-            out_specs=pl.BlockSpec((1, three, rows, width), lambda i, source_ref: (i, 0, 0, 0)),
+            grid=(count, number),
+            in_specs=in_specs,
+            out_specs=pl.BlockSpec(block, lambda i, p, source_ref: (i, p + first, 0, 0)),
         ),
+        input_output_aliases={} if held is None else {2: 0},
         compiler_params=pltpu.CompilerParams(vmem_limit_bytes=24 * 2**20),
-    )(source, moved)
+        cost_estimate=pl.CostEstimate(
+            flops=0, bytes_accessed=2 * moved.size * 2, transcendentals=0
+        ),
+    )(*operands)
 
 
 def per_device(
@@ -113,6 +141,9 @@
     column_width = attn_weight.shape[1]
     capacity = max(2, (7 * row_count * routes.shape[1] + 6 * mp_count - 1) // (6 * mp_count))
 
+    first_piece, second_piece, context = lax.optimization_barrier(
+        (cut_piece(weights, PARTS[0][0]), cut_piece(weights, PARTS[1][0]), context)
+    )
     whole_context = lax.all_gather(context, "dp", axis=0, tiled=True)
     partial_value = jnp.dot(whole_context, attn_weight, preferred_element_type=jnp.float32)
     partial_value = partial_value.astype(jnp.bfloat16).reshape(-1, row_count, column_width)
@@ -129,10 +160,11 @@
     wide_ids = jnp.arange(-(-mp_count // 128) * 128, dtype=jnp.int32)
     naming = jnp.any(routes[:, :, None] == wide_ids[None, None, :], axis=1).astype(jnp.bfloat16)
     packet = jnp.concatenate([normed, naming], axis=1)
-    packet, weights = lax.optimization_barrier((packet, weights))
+    packet, early = lax.optimization_barrier((packet, send_ahead(first_piece)))
     packets = lax.all_gather(packet, ("dp", "mp"), axis=0, tiled=True)
-    moved = move(weights, None, PARTS[0], 0)
-    packets, moved = lax.optimization_barrier((packets, moved))
+    moved = move(weights, early, PARTS[0], 0)
+    packets, moved, second_piece = lax.optimization_barrier((packets, moved, second_piece))
+    early = send_ahead(second_piece)
 
     contract = (((1,), (1,)), ((), ()))
     mine = inference_slot[me] == expert_ids
@@ -156,9 +188,11 @@
     active = (jax.nn.silu(gate) * up).astype(jnp.bfloat16)
     answers = jnp.dot(active, experts[2], preferred_element_type=jnp.float32)
     answers = answers.astype(jnp.bfloat16).reshape(groups, capacity, model_width)
+    answers, early = lax.optimization_barrier((answers, early))
     returned = lax.all_to_all(answers, ("dp", "mp"), split_axis=0, concat_axis=0, tiled=True)
-    returned, moved = lax.optimization_barrier((returned, moved))
-    moved = move(weights, moved, PARTS[1], 1)
+    held = place(moved, source, PARTS[0], None)
+    returned, held, early = lax.optimization_barrier((returned, held, early))
+    moved = move(weights, early, PARTS[1], 1)
 
     logits = lax.dot_general(normed, router_weight, contract, preferred_element_type=jnp.float32)
     matches = naming[:, :mp_count] > 0
@@ -175,7 +209,7 @@
         returned.astype(jnp.float32).reshape(dp_count, -1, model_width), axis=0
     )
     mix = jnp.dot(mixing.T, results, precision=lax.Precision.HIGHEST).astype(jnp.bfloat16)
-    return (hidden, mix, place(moved, source))
+    return (hidden, mix, place(moved, source, PARTS[1], held))
 
 
 def slot_picks(named, capacity):

time: 635 us -> 618 us (0.973)
  Pallas kernels: 535 us -> 504 us
  waiting for transfers between devices: 31.1 us -> 40.3 us
    pallas_call x3 -> x4, Pallas kernels: 535 us -> 504 us  [the longest x2 483 us: move(): pl.pallas_call(functools.partial(move_kernel, parts, parts[0]), out_shape...]
    ppermute x0 -> x2, waiting for transfers between devices: none -> 15.4 us  [send_ahead(): lax.ppermute(piece, 'mp', [(i, (i + half) % count) for i in range(count)])]
    all_to_all x1, waiting for transfers between devices: 15.2 us -> 0.01 us  [per_device(): lax.all_to_all(answers, ('dp', 'mp'), split_axis=0, concat_axis=0, tiled=...]
    all_to_all x1, waiting for transfers between devices: 15.8 us -> 24.9 us  [per_device(): lax.all_to_all(partial_value, ('dp', 'mp'), split_axis=0, concat_axis=0,...]
  transfers between devices with their start and end apart: 3 -> 5, of which waited for: 2 -> 3; matrix products, arithmetic and copies ran while one was open for 1% -> 3% of each run, Pallas kernels for 55% -> 56%
where the time goes in v2:
time: 618 us
  Pallas kernels  504 us (82%)
  waiting for transfers between devices  40.3 us (7%)
  local copies, waits for them, and re-layouts  18.3 us (3%)
  matrix products  18.3 us (3%)
  starting transfers between devices  16 us (3%)
  between operations  14.3 us (2%)
    pallas_call x2, Pallas kernels, move(): pl.pallas_call(functools.partial(move_kernel, parts, parts[0]), out_shape...  483 us
    all_to_all x1, waiting for transfers between devices, per_device(): lax.all_to_all(partial_value, ('dp', 'mp'), split_axis=0, concat_axis=0,...  24.9 us
    pallas_call x2, Pallas kernels, place(): pl.pallas_call(place_kernel, out_shape=jax.ShapeDtypeStruct((count, 3, ro...  20.9 us
    ppermute x2, waiting for transfers between devices, send_ahead(): lax.ppermute(piece, 'mp', [(i, (i + half) % count) for i in range(count)])  15.4 us
  transfers between devices with their start and end apart: 5, of which 3 were waited for; matrix products, arithmetic and copies ran while one was open for 3% of the time, Pallas kernels for 56%

profile of v2, /device:TPU:11, one launch (start us, length us, event | category | flops | bytes accessed | tf_op | source)
XLA Modules:
  0.0 618.0 jit_solution(2566491169619863671)
XLA Ops:
  7.2 2.3 dynamic-slice_bitcast_fusion
  9.6 4.0 all_gather.6
  14.1 1.0 reshape.130
  15.1 7.5 %all-to-all-start = ((bf16[32,4,2560]{2,1,0:T(4,128)(2,1)}), bf16[32,4,2560]{2,1,0:T(4,128)(2,1)S(1)}, u32[]{:S(2)}, u32[]{:S(2)}) async-start(bf16[32,4,2560]{2,1,0:T(4,128)(2,1)} %reshape.130), calls=%async_computation | async-start | bytes 1310720 | tf_op jit(solution)/shard_map/all_to_all | solution.py:150
  22.6 2.2 collective-permute-start
  25.0 24.9 %all-to-all-done = bf16[32,4,2560]{2,1,0:T(4,128)(2,1)S(1)} async-done(((bf16[32,4,2560]{2,1,0:T(4,128)(2,1)}), bf16[32,4,2560]{2,1,0:T(4,128)(2,1)S(1)}, u32[]{:S(2)}, u32[]{:S(2)}) %all-to-all-start) | async-done | bytes 655392 | tf_op jit(solution)/shard_map/all_to_all | solution.py:150
  50.5 0.6 pad_maximum_fusion
  51.1 7.2 %collective-permute-done.early = bf16[48,5120]{1,0:T(8,128)(2,1)S(1)} collective-permute-done((bf16[48,5120]{1,0:T(8,128)(2,1)}, bf16[48,5120]{1,0:T(8,128)(2,1)S(1)}, u32[]{:S(2)}, u32[]{:S(2)}) %collective-permute-start) | collective-permute-done | bytes 491552 | tf_op jit(solution)/shard_map/ppermute | solution.py:96
  58.4 0.6 dynamic_slice.11
  59.0 0.6 iota_compare_fusion.4
  59.7 329.9 %shard_map.103.refs_1_ = bf16[16,2,48,5120]{3,2,1,0:T(8,128)(2,1)} custom-call(bf16[3,16,48,5120]{3,2,1,0:T(8,128)(2,1)} %bitcast.45, bf16[48,5120]{1,0:T(8,128)(2,1)} %copy-done.6), custom_call_target="tpu_custom_call" | custom-call | bytes 1258291200 | tf_op jit(solution)/shard_map/pallas_call | solution.py:71
  389.6 2.5 reshape.142
  392.9 0.8 and.79
  394.0 5.7 fusion.4
  399.9 10.4 %fusion.9 = bf16[64,5120]{1,0:T(8,128)(2,1)S(1)} fusion(bf16[1,3,768,5120]{3,2,1,0:T(8,128)(2,1)} %param.13, bf16[64,5120]{1,0:T(8,128)(2,1)S(1)} %convolution_convert_fusion, f32[64,768]{1,0:T(8,128)S(1)} %fusion.4), kind=kOutput, calls=%fused_computation.9 | convolution fusion | flops 1007255552 | bytes 17235968 | tf_op jit(solution)/shard_map/dot_general | solution.py:189
  410.3 1.1 reshape.134
  411.4 8.1 %collective-permute-done.1.early = bf16[48,5120]{1,0:T(8,128)(2,1)S(1)} collective-permute-done((bf16[48,5120]{1,0:T(8,128)(2,1)S(1)}, bf16[48,5120]{1,0:T(8,128)(2,1)S(1)}, u32[]{:S(2)}, u32[]{:S(2)}) %collective-permute-start.1) | collective-permute-done | bytes 491552 | tf_op jit(solution)/shard_map/ppermute | solution.py:96
  419.5 6.2 %all-to-all-start.1 = ((bf16[32,2,5120]{2,1,0:T(2,128)(2,1)}), bf16[32,2,5120]{2,1,0:T(2,128)(2,1)S(1)}, u32[]{:S(2)}, u32[]{:S(2)}) async-start(bf16[32,2,5120]{2,1,0:T(2,128)(2,1)} %reshape.134), calls=%async_computation.1 | async-start | bytes 1310720 | tf_op jit(solution)/shard_map/all_to_all | solution.py:192
  427.3 5.5 copy-done.2
  432.8 13.7 %shard_map.104.refs_2_ = bf16[16,3,48,5120]{3,2,1,0:T(8,128)(2,1)} custom-call(s32[16]{0:T(128)S(1)} %select_reduce_fusion.1.refs_0_, bf16[16,2,48,5120]{3,2,1,0:T(8,128)(2,1)S(1)} %copy-done.2), custom_call_target="tpu_custom_call" | custom-call | bytes 31457280 | tf_op jit(solution)/shard_map/pallas_call | solution.py:112
  446.6 152.9 %shard_map.105.refs_1_ = bf16[16,1,48,5120]{3,2,1,0:T(8,128)(2,1)} custom-call(bf16[3,16,48,5120]{3,2,1,0:T(8,128)(2,1)} %bitcast.46, bf16[48,5120]{1,0:T(8,128)(2,1)} %copy-done.4), custom_call_target="tpu_custom_call" | custom-call | bytes 629145600 | tf_op jit(solution)/shard_map/pallas_call | solution.py:71
  599.7 3.2 copy-done.3
  602.9 7.2 %shard_map.106 = bf16[16,3,48,5120]{3,2,1,0:T(8,128)(2,1)} custom-call(s32[16]{0:T(128)S(1)} %select_reduce_fusion.1.refs_0_, bf16[16,1,48,5120]{3,2,1,0:T(8,128)(2,1)S(1)} %copy-done.3, bf16[16,3,48,5120]{3,2,1,0:T(8,128)(2,1)} %shard_map.104.refs_2_), custom_call_target="tpu_custom_call", output_to_operand_aliasing={{}: (2, {})} | custom-call | bytes 15728640 | tf_op jit(solution)/shard_map/pallas_call | solution.py:112
  610.1 1.0 convolution_convert_fusion.1
  (69 shorter events, 4.4 us)
Async XLA Ops:
  7.2 6.4 %copy-start = (bf16[512,2560]{1,0:T(8,128)(2,1)S(1)}, bf16[512,2560]{1,0:T(8,128)(2,1)}, u32[]{:S(2)}) copy-start(bf16[512,2560]{1,0:T(8,128)(2,1)} %param.9) | copy-start | bytes 7864324
  7.2 17.6 %copy-start.10 = (s32[4,6]{1,0:T(4,128)S(1)}, s32[4,6]{1,0:T(4,128)}, u32[]{:S(2)}) copy-start(s32[4,6]{1,0:T(4,128)} %param.15) | copy-start | bytes 292
  7.2 43.0 %copy-start.8 = (bf16[4,5120]{1,0:T(4,128)(2,1)S(1)}, bf16[4,5120]{1,0:T(4,128)(2,1)}, u32[]{:S(2)}) copy-start(bf16[4,5120]{1,0:T(4,128)(2,1)} %param.10) | copy-start | bytes 122884
  7.2 43.2 %copy-start.9 = (f32[5120]{0:T(1024)S(1)}, f32[5120]{0:T(1024)}, u32[]{:S(2)}) copy-start(f32[5120]{0:T(1024)} %param.11) | copy-start | bytes 61444
  7.2 51.2 %copy-start.11 = (s32[16]{0:T(128)S(1)}, s32[16]{0:T(128)}, u32[]{:S(2)}) copy-start(s32[16]{0:T(128)} %param.14) | copy-start | bytes 196
  15.1 34.8 %all-to-all-start = ((bf16[32,4,2560]{2,1,0:T(4,128)(2,1)}), bf16[32,4,2560]{2,1,0:T(4,128)(2,1)S(1)}, u32[]{:S(2)}, u32[]{:S(2)}) async-start(bf16[32,4,2560]{2,1,0:T(4,128)(2,1)} %reshape.130), calls=%async_computation | async-start | bytes 1310720 | tf_op jit(solution)/shard_map/all_to_all | solution.py:150
  22.6 367.0 %all-gather.3.cloned.1.call-start = ((), (), s32[]{:S(2)}) async-start(), calls=%async_computation.2 | async-start | bytes 1385472 | tf_op jit(solution)/shard_map/all_gather | solution.py:164
  22.6 35.7 %collective-permute-start = (bf16[48,5120]{1,0:T(8,128)(2,1)}, bf16[48,5120]{1,0:T(8,128)(2,1)S(1)}, u32[]{:S(2)}, u32[]{:S(2)}) collective-permute-start(bf16[48,5120]{1,0:T(8,128)(2,1)} %get-tuple-element.17), channel_id=1, source_target_pairs={{0,8},{1,9},{2,10},{3,11},{4,12},{5,13},{6,14},{7,15},{8,0},{9,1},... | collective-permute-start | bytes 1474568 | tf_op jit(solution)/shard_map/ppermute | solution.py:96
  50.3 339.2 %copy-start.7 = (bf16[4,5120]{1,0:T(4,128)(2,1)}, bf16[4,5120]{1,0:T(4,128)(2,1)S(1)}, u32[]{:S(2)}) copy-start(bf16[4,5120]{1,0:T(4,128)(2,1)S(1)} %get-tuple-element.30) | copy-start | bytes 122884
  58.4 1.4 copy-start.6
  389.6 10.2 %copy-start.5 = (bf16[48,5120]{1,0:T(8,128)(2,1)S(1)}, bf16[48,5120]{1,0:T(8,128)(2,1)}, u32[]{:S(2)}) copy-start(bf16[48,5120]{1,0:T(8,128)(2,1)} %get-tuple-element.22) | copy-start | bytes 1474564
  399.8 26.9 %copy-start.12 = (bf16[16,5120]{1,0:T(8,128)(2,1)S(1)}, bf16[16,5120]{1,0:T(8,128)(2,1)}, u32[]{:S(2)}) copy-start(bf16[16,5120]{1,0:T(8,128)(2,1)} %param.12) | copy-start | bytes 491524
  399.8 19.7 %collective-permute-start.1 = (bf16[48,5120]{1,0:T(8,128)(2,1)S(1)}, bf16[48,5120]{1,0:T(8,128)(2,1)S(1)}, u32[]{:S(2)}, u32[]{:S(2)}) collective-permute-start(bf16[48,5120]{1,0:T(8,128)(2,1)S(1)} %copy-done.5), channel_id=1, source_target_pairs={{0,8},{1,9},{2,10},{3,11},{4,12},{5,13},{6,14},{7,15},{8,0},{9,1},... | collective-permute-start | bytes 1474568 | tf_op jit(solution)/shard_map/ppermute | solution.py:96
  419.5 26.9 %copy-start.4 = (bf16[48,5120]{1,0:T(8,128)(2,1)}, bf16[48,5120]{1,0:T(8,128)(2,1)S(1)}, u32[]{:S(2)}) copy-start(bf16[48,5120]{1,0:T(8,128)(2,1)S(1)} %collective-permute-done.1.early) | copy-start | bytes 1474564
  419.5 26.9 %all-to-all-start.1 = ((bf16[32,2,5120]{2,1,0:T(2,128)(2,1)}), bf16[32,2,5120]{2,1,0:T(2,128)(2,1)S(1)}, u32[]{:S(2)}, u32[]{:S(2)}) async-start(bf16[32,2,5120]{2,1,0:T(2,128)(2,1)} %reshape.134), calls=%async_computation.1 | async-start | bytes 1310720 | tf_op jit(solution)/shard_map/all_to_all | solution.py:192
  427.3 5.5 copy-start.2
  599.7 3.2 copy-start.3
  602.9 8.3 %copy-start.1 = (bf16[512,2560]{1,0:T(8,128)(2,1)S(1)}, bf16[512,2560]{1,0:T(8,128)(2,1)}, u32[]{:S(2)}) copy-start(bf16[512,2560]{1,0:T(8,128)(2,1)} %param.9) | copy-start | bytes 7864324
Sparse Core Ops, SparseCore 0:
  58.5 267.1 all-gather.2
